TPU v7x, 32 devices: a whole 2x2x4 slice. The times are simulated.
32 devices in a mesh: tok: 8 (over y, x, core), mdl: 4 (over z).
Axes of the slice: x: 2, y: 2, z: 4, core: 2. Of those that a mesh axis runs over, the one named last changes fastest.
Arguments:
- hidden: bfloat16 [4096, 2048], P('tok'), may hold values from -40 to 40
- segment_ids: int32 [4096], replicated, may hold values from 0 to 3, never falling along the last dimension, each value on 1 to 2048 neighbouring positions
- routes: int32 [4096, 2], P('tok'), may hold values from 0 to 7, all different within a row; in each aligned block of 512 rows (0 to 511, 512 to 1023, ...) at most 256 rows name the same one
- norm_gain: float32 [2048], replicated, may hold values from 0.5 to 1.5
- router_weight: float32 [2048, 8], replicated, may hold values from -0.125 to 0.125
- query_weight: bfloat16 [8, 2048, 2048], P(None, 'tok', 'mdl'), may hold values from -2 to 2
- kv_weight: bfloat16 [2, 2048, 2048], P(None, 'tok', 'mdl'), may hold values from -16 to 16
- out_weight: bfloat16 [8, 2048, 2048], P(None, 'mdl', 'tok'), may hold values from -0.5 to 0.5
- page_table: int32 [256], P('tok'), may hold values from 0 to 255, as said below
Outputs:
- output: bfloat16 [4096, 2048], P('tok', 'mdl')
- cache: bfloat16 [256, 16, 2, 2048], P('tok', None, None, 'mdl')
Inputs may be any that keep to these rules, and one draw needn't show every extreme that they name: `segment_ids`: Non-decreasing along the tokens; every prompt number 0 to 3 occurs, each prompt 1 to 2048 tokens long, one exactly 2048. `routes`: each token names 2 different experts; among the 512 tokens of an aligned block no expert is named more than 256 times, and some block reaches 256. `page_table`: A permutation of the 256 physical pages; of the 32 logical pages of each aligned block, exactly 4 lie in each aligned range of 32 physical pages.
All inputs are finite; a program needn't handle non-finite values.
Results may differ from a plain program's by a relative error of at most 0.019.
Values may be sent and summed in bfloat16 or wider, within the bound.
A program may use at most 128 MiB of HBM per device.

v0:
```python
import math

import jax
import jax.numpy as jnp
from jax import lax
from jax.sharding import PartitionSpec as P

HDIM = 128
SEGS = 4


EPSILON = 1e-05
MASKED = -1e30


def rms_norm(hidden, norm_gain):
    values = hidden.astype(jnp.float32)
    factor = lax.rsqrt(jnp.mean(values * values, axis=-1, keepdims=True) + EPSILON)
    return (values * factor * norm_gain).astype(jnp.bfloat16)


def route_gates(normed, router_weight, routes):
    logits = jnp.dot(normed.astype(jnp.float32), router_weight, precision=lax.Precision.HIGHEST)
    expert_ids = jnp.arange(logits.shape[1], dtype=jnp.int32)
    picked = routes[:, :, None] == expert_ids[None, None, :]
    chosen = jnp.sum(jnp.where(picked, logits[:, None, :], jnp.float32(0.0)), axis=-1)
    return jax.nn.softmax(chosen, axis=-1)


def place_pages(key_values, page_table, shards, tok_row):
    pages_here = page_table.shape[0]
    per_peer = pages_here // shards
    page_rows = key_values.shape[0] // pages_here
    head_cols = key_values.shape[2]
    targets = page_table // pages_here
    onehot = (targets[:, None] == jnp.arange(shards, dtype=jnp.int32)[None, :]).astype(jnp.int32)
    ranks = jnp.sum((jnp.cumsum(onehot, axis=0) - 1) * onehot, axis=1)
    ordering = (
        jnp.zeros((pages_here,), jnp.int32)
        .at[targets * per_peer + ranks]
        .set(jnp.arange(pages_here, dtype=jnp.int32))
    )
    outgoing = key_values.reshape(pages_here, page_rows, 2, head_cols)[ordering].reshape(
        shards, per_peer, page_rows, 2, head_cols
    )
    labels = page_table[ordering].reshape(shards, per_peer)
    incoming, got_labels = (
        lax.all_to_all(outgoing, "tok", split_axis=0, concat_axis=0, tiled=True),
        lax.all_to_all(labels, "tok", split_axis=0, concat_axis=0, tiled=True),
    )
    places = got_labels.reshape(-1) - tok_row * pages_here
    arrived = incoming.reshape(pages_here, page_rows, 2, head_cols)
    return jnp.zeros((pages_here, page_rows, 2, head_cols), jnp.bfloat16).at[places].set(arrived)


def local(
    hidden,
    segment_ids,
    routes,
    norm_gain,
    router_weight,
    query_weight,
    kv_weight,
    out_weight,
    page_table,
):
    tok_dev, width = hidden.shape
    experts = query_weight.shape[0]
    head_cols = query_weight.shape[2]
    heads_here = head_cols // HDIM
    capacity = tok_dev // 2
    top_count = routes.shape[1]
    assigned = tok_dev * top_count
    shards = lax.axis_size("tok")
    tok_row = lax.axis_index("tok")
    normed = rms_norm(hidden, norm_gain)
    gates = route_gates(normed, router_weight, routes)
    flat_expert = routes.reshape(-1)
    expert_ids = jnp.arange(experts, dtype=jnp.int32)
    onehot = (flat_expert[:, None] == expert_ids[None, :]).astype(jnp.int32)
    ranks = jnp.sum((jnp.cumsum(onehot, axis=0) - 1) * onehot, axis=1)
    slots = flat_expert * capacity + ranks
    assign_ids = jnp.arange(assigned, dtype=jnp.int32)
    slot_assign = jnp.zeros((experts * capacity,), jnp.int32).at[slots].set(assign_ids)
    slot_token = slot_assign // top_count
    slot_filled = jnp.zeros((experts * capacity,), jnp.bfloat16).at[slots].set(jnp.bfloat16(1.0))
    slot_gate = jnp.zeros((experts * capacity,), jnp.float32).at[slots].set(gates.reshape(-1))
    grouped = (normed[slot_token] * slot_filled[:, None]).reshape(experts, capacity, width)
    query_part = lax.all_gather(query_weight, "tok", axis=1, tiled=True)
    key_part = lax.all_gather(kv_weight, "tok", axis=1, tiled=True)
    query_total = jnp.einsum(
        "ecd,edh->ech", grouped, query_part, preferred_element_type=jnp.float32
    )
    key_total = jnp.einsum("td,kdh->tkh", normed, key_part, preferred_element_type=jnp.float32)
    queries = query_total.astype(jnp.bfloat16).reshape(experts * capacity, head_cols)[slots]
    key_values = key_total.astype(jnp.bfloat16)
    cache = place_pages(key_values, page_table, shards, tok_row)
    by_head_q = queries.reshape(assigned, heads_here, HDIM).transpose(1, 0, 2)
    q_pos = tok_row * tok_dev + assign_ids // top_count
    q_seg = segment_ids[q_pos]
    prompt_ids = jnp.arange(SEGS, dtype=jnp.int32)
    seg_first = jnp.sum((segment_ids[:, None] < prompt_ids[None, :]).astype(jnp.int32), axis=0)
    q_lower = jnp.sum(
        jnp.where(q_seg[:, None] == prompt_ids[None, :], seg_first[None, :], 0), axis=1
    )
    start_state = (
        jnp.full((heads_here, assigned), MASKED, jnp.float32),
        jnp.zeros((heads_here, assigned), jnp.float32),
        jnp.zeros((heads_here, assigned, HDIM), jnp.float32),
    )
    state = start_state
    piece = lax.all_gather(key_values, "tok", axis=0, tiled=True)
    count = piece.shape[0]
    block = math.gcd(count, 512)
    key_blocks = piece[:, 0].reshape(count // block, block, heads_here, HDIM)
    value_blocks = piece[:, 1].reshape(count // block, block, heads_here, HDIM)
    firsts = block * jnp.arange(count // block, dtype=jnp.int32)

    def one_block(carry, inputs):
        peak, total, accum = carry
        key_block, value_block, first = inputs
        k_pos = first + jnp.arange(block, dtype=jnp.int32)
        allowed = (k_pos[None, :] >= q_lower[:, None]) & (k_pos[None, :] <= q_pos[:, None])
        scores = jnp.einsum(
            "hqd,khd->hqk", by_head_q, key_block, preferred_element_type=jnp.float32
        ) / math.sqrt(HDIM)
        scores = jnp.where(allowed[None], scores, jnp.float32(MASKED))
        new_peak = jnp.maximum(peak, jnp.max(scores, axis=-1))
        shrink = jnp.exp(peak - new_peak)
        expon = jnp.where(allowed[None], jnp.exp(scores - new_peak[..., None]), jnp.float32(0.0))
        total = total * shrink + jnp.sum(expon, axis=-1)
        accum = accum * shrink[..., None] + jnp.einsum(
            "hqk,khd->hqd",
            expon.astype(jnp.bfloat16),
            value_block,
            preferred_element_type=jnp.float32,
        )
        return ((new_peak, total, accum), None)

    state, _ = lax.scan(one_block, state, (key_blocks, value_blocks, firsts))
    attended = (
        (state[2] / state[1][..., None])
        .astype(jnp.bfloat16)
        .transpose(1, 0, 2)
        .reshape(assigned, head_cols)
    )
    grouped_out = (attended[slot_assign] * slot_filled[:, None]).reshape(
        experts, capacity, head_cols
    )
    piece = lax.all_gather(out_weight, "tok", axis=2, tiled=True)
    count = piece.shape[2]
    terms = jnp.einsum(
        "ech,ehn->ecn", grouped_out, piece, preferred_element_type=jnp.float32
    ).reshape(experts * capacity, count)
    partial_sums = (
        jnp.zeros((tok_dev, count), jnp.float32).at[slot_token].add(terms * slot_gate[:, None])
    )
    mine = lax.psum_scatter(
        partial_sums.astype(jnp.bfloat16), "mdl", scatter_dimension=1, tiled=True
    ).astype(jnp.float32)
    span = width // lax.axis_size("mdl")
    residual_part = lax.dynamic_slice_in_dim(hidden, lax.axis_index("mdl") * span, span, 1)
    output = (residual_part.astype(jnp.float32) + mine).astype(jnp.bfloat16)
    return (output, cache)


def solution(mesh):
    placed = (
        P("tok", None),
        P(),
        P("tok", None),
        P(),
        P(),
        P(None, "tok", "mdl"),
        P(None, "tok", "mdl"),
        P(None, "mdl", "tok"),
        P("tok"),
    )
    return jax.shard_map(
        local,
        mesh=mesh,
        in_specs=placed,
        out_specs=(P("tok", "mdl"), P("tok", None, None, "mdl")),
        check_vma=False,
    )
```

profile of v0, /device:TPU:0, one launch (start us, length us, event | category | flops | bytes accessed | tf_op | source)
XLA Modules:
  0.0 500.0 jit_solution(15416829478685200710)
XLA Ops:
  12.2 37.2 %all-gather.5.cloned.1.call-done = bf16[2,2048,512]{2,1,0:T(8,128)(2,1)} async-done(((bf16[2,256,512]{2,1,0:T(8,128)(2,1)}), bf16[2,2048,512]{2,1,0:T(8,128)(2,1)}) %all-gather.5.cloned.1.call-update) | async-done | bytes 4194320 | tf_op jit(solution)/shard_map/all_gather | solution.py:90
  49.4 5.5 %fusion.35 = bf16[512,2,512]{2,0,1:T(8,128)(2,1)} fusion(bf16[2,2048,512]{2,1,0:T(8,128)(2,1)} %all-gather.5.cloned.1.call-done, bf16[512,2048]{1,0:T(8,128)(2,1)S(1)} %fusion.24), kind=kOutput, calls=%fused_computation.61 | convolution fusion | flops 2148007936 | bytes 7340032 | tf_op jit(solution)/shard_map/td,kdh->tkh/dot_general | solution.py:94
  60.0 4.3 scatter_custom_fusion
  64.4 10.9 %gather_fusion.1 = bf16[2048,2048]{1,0:T(8,128)(2,1)} fusion(bf16[512,2048]{1,0:T(8,128)(2,1)S(1)} %fusion.24, s32[2048]{0:T(1024)S(1)} %get-tuple-element.163), kind=kCustom, calls=%fused_computation.1 | custom fusion | bytes 16785408 | tf_op jit(solution)/shard_map/gather | solution.py:88
  75.3 7.6 %scatter_custom_fusion.1 = bf16[2048]{0:T(1024)(128)(2,1)S(1)} fusion(s32[1024]{0:T(1024)S(1)} %bitcast.101, bf16[1024]{0:T(1024)(128)(2,1)S(1)} %broadcast.274, bf16[]{:T(256)} %constant.112.clone.1), kind=kCustom, calls=%fused_computation.116 | custom fusion | bytes 4098 | tf_op jit(solution)/shard_map/scatter | solution.py:86
  83.1 6.1 %gather_fusion = s32[1024]{0:T(1024)S(1)} fusion(s32[4096]{0:T(1024)S(1)} %copy-done.2, s32[1024]{0:T(1024)S(1)} %broadcast_clamp_fusion.2), kind=kCustom, calls=%fused_computation | custom fusion | bytes 12288 | tf_op jit(solution)/shard_map/gather | solution.py:100
  91.5 4.5 scatter_custom_fusion.2
  96.0 13.4 %all-gather.7.cloned.1.call-done = bf16[4096,2,512]{2,0,1:T(8,128)(2,1)} async-done(((bf16[512,2,512]{2,0,1:T(8,128)(2,1)}), bf16[4096,2,512]{2,0,1:T(8,128)(2,1)}) %all-gather.7.cloned.1.call-update) | async-done | bytes 8388624 | tf_op jit(solution)/shard_map/all_gather | solution.py:112
  109.4 5.7 %fusion.59 = (bf16[4096,1,512]{2,0,1:T(8,128)(2,1)}, bf16[4096,1,512]{2,0,1:T(8,128)(2,1)}) fusion(bf16[4096,2,512]{2,0,1:T(8,128)(2,1)} %all-gather.7.cloned.1.call-done), kind=kLoop, calls=%fused_computation.128 | loop fusion | bytes 16777216 | tf_op jit(solution)/shard_map/slice | solution.py:116
  115.1 7.1 %reshape_squeeze.6 = bf16[8,512,4,128]{3,2,1,0:T(4,128)(2,1)} reshape(bf16[4096,1,512]{2,0,1:T(8,128)(2,1)} %get-tuple-element.170) | data formatting | bytes 8388608 | tf_op jit(solution)/shard_map/reshape;squeeze | solution.py:115
  122.3 7.1 %reshape_squeeze.7 = bf16[8,512,4,128]{3,2,1,0:T(4,128)(2,1)} reshape(bf16[4096,1,512]{2,0,1:T(8,128)(2,1)} %get-tuple-element.169) | data formatting | bytes 8388608 | tf_op jit(solution)/shard_map/reshape;squeeze | solution.py:116
  129.3 72.1 %all-gather.9.cloned.1.call-done = bf16[8,2048,512]{2,1,0:T(8,128)(2,1)} async-done(((bf16[8,256,512]{2,1,0:T(8,128)(2,1)}), bf16[8,2048,512]{2,1,0:T(8,128)(2,1)}) %all-gather.9.cloned.1.call-update) | async-done | bytes 16777232 | tf_op jit(solution)/shard_map/all_gather | solution.py:89
  201.4 12.7 %fusion.32 = bf16[8,256,512]{2,1,0:T(8,128)(2,1)S(1)} fusion(bf16[8,2048,512]{2,1,0:T(8,128)(2,1)} %all-gather.9.cloned.1.call-done, bf16[8,256,2048]{2,1,0:T(8,128)(2,1)} %bitcast.94, bf16[8,256]{1,0:T(8,128)(2,1)S(1)} %mul.110), kind=kOutput, calls=%fused_computation.60 | convolution fusion | flops 4300210176 | bytes 27267072 | tf_op jit(solution)/shard_map/ecd,edh->ech/dot_general | solution.py:91
  214.1 4.0 gather_fusion.2
  218.2 160.6 %while.15 = (s32[]{:T(128)}, f32[4,1024]{1,0:T(4,128)S(1)}, f32[4,1024]{1,0:T(4,128)S(1)}, f32[4,1024,128]{2,1,0:T(8,128)}, s32[8]{0:T(128)S(1)}, /*index=5*/s32...) while((s32[]{:T(128)}, f32[4,1024]{1,0:T(4,128)S(1)}, ...), condition=%wide.region_11.12_spmd.clone, body=%wide.region_8.11_spmd.clone.sunk | while | flops 1104180736 | bytes 69484728 | solution.py:140
  221.5 4.9 fusion.79
  226.5 4.7 fusion.80
  232.3 4.5 fusion.82
  240.1 6.3 %fusion.79 = (f32[4,1024]{1,0:T(4,128)S(1)}, f32[4,512,1024]{2,1,0:T(8,128)}) fusion(pred[1024,512]{0,1:T(8,128)(4,1)S(1)} %compare_and_fusion.2, bf16[4,1024,128]{2,1,0:T(8,128)(2,1)S(1)} %get-tuple-element.276, bf16[1,512,4,128]{3,2,1,0:T(4,128)(2,1)S(1)} %get-tuple-element.239), kind=kOutput, calls=%fused_computation.15.clone.1 | convolution fusion | flops 543158272 | bytes 10502144 | tf_op jit(solution)/shard_map/while/body/eval_jaxpr/hqd,khd->hqk/dot_general | solution.py:124
  246.5 5.0 %fusion.80 = f32[4,1024]{1,0:T(4,128)S(1)} fusion(f32[4,512,1024]{2,1,0:T(8,128)} %get-tuple-element.241, f32[4,1024]{1,0:T(4,128)S(1)} %select_maximum_fusion.2, pred[1024,512]{0,1:T(8,128)(4,1)S(1)} %compare_and_fusion.2), kind=kLoop, calls=%fused_computation.17.clone.1 | loop fusion | flops 10481664 | bytes 8945664 | tf_op jit(solution)/shard_map/while/body/eval_jaxpr/reduce_sum | solution.py:131
  253.0 5.8 %fusion.82 = f32[4,1024,128]{2,1,0:T(8,128)} fusion(f32[4,1024,128]{2,1,0:T(8,128)} %get-tuple-element.260, f32[4,512,1024]{2,1,0:T(8,128)S(1)} %copy-done.3, f32[4,1024]{1,0:T(4,128)S(1)} %select_maximum_fusion.2, pred[1024,512]{0,1:T(8,128)(4,1)S(1)} %compare_and_fusion.2, f32[4,1024]{1,0:T(4,128)S(1)} %get-tuple-element.243, pred[]{:T(512)S(6)} %compare.11, ...), kind=kOutput, calls=%fused_computation.21.clone.1 | convolution fusion | flops 548929536 | bytes 13664257 | tf_op jit(solution)/shard_map/while/body/eval_jaxpr/hqk,khd->hqd/dot_general | solution.py:132
  262.1 4.9 fusion.79
  267.0 5.0 %fusion.80 = f32[4,1024]{1,0:T(4,128)S(1)} fusion(f32[4,512,1024]{2,1,0:T(8,128)} %get-tuple-element.241, f32[4,1024]{1,0:T(4,128)S(1)} %select_maximum_fusion.2, pred[1024,512]{0,1:T(8,128)(4,1)S(1)} %compare_and_fusion.2), kind=kLoop, calls=%fused_computation.17.clone.1 | loop fusion | flops 10481664 | bytes 8945664 | tf_op jit(solution)/shard_map/while/body/eval_jaxpr/reduce_sum | solution.py:131
  273.2 5.7 %fusion.82 = f32[4,1024,128]{2,1,0:T(8,128)} fusion(f32[4,1024,128]{2,1,0:T(8,128)} %get-tuple-element.260, f32[4,512,1024]{2,1,0:T(8,128)S(1)} %copy-done.3, f32[4,1024]{1,0:T(4,128)S(1)} %select_maximum_fusion.2, pred[1024,512]{0,1:T(8,128)(4,1)S(1)} %compare_and_fusion.2, f32[4,1024]{1,0:T(4,128)S(1)} %get-tuple-element.243, pred[]{:T(512)S(6)} %compare.11, ...), kind=kOutput, calls=%fused_computation.21.clone.1 | convolution fusion | flops 548929536 | bytes 13664257 | tf_op jit(solution)/shard_map/while/body/eval_jaxpr/hqk,khd->hqd/dot_general | solution.py:132
  282.2 4.9 fusion.79
  287.1 4.7 fusion.80
  294.0 5.8 %fusion.82 = f32[4,1024,128]{2,1,0:T(8,128)} fusion(f32[4,1024,128]{2,1,0:T(8,128)} %get-tuple-element.260, f32[4,512,1024]{2,1,0:T(8,128)S(1)} %copy-done.3, f32[4,1024]{1,0:T(4,128)S(1)} %select_maximum_fusion.2, pred[1024,512]{0,1:T(8,128)(4,1)S(1)} %compare_and_fusion.2, f32[4,1024]{1,0:T(4,128)S(1)} %get-tuple-element.243, pred[]{:T(512)S(6)} %compare.11, ...), kind=kOutput, calls=%fused_computation.21.clone.1 | convolution fusion | flops 548929536 | bytes 13664257 | tf_op jit(solution)/shard_map/while/body/eval_jaxpr/hqk,khd->hqd/dot_general | solution.py:132
  303.0 4.9 fusion.79
  307.9 4.7 fusion.80
  313.8 5.8 %fusion.82 = f32[4,1024,128]{2,1,0:T(8,128)} fusion(f32[4,1024,128]{2,1,0:T(8,128)} %get-tuple-element.260, f32[4,512,1024]{2,1,0:T(8,128)S(1)} %copy-done.3, f32[4,1024]{1,0:T(4,128)S(1)} %select_maximum_fusion.2, pred[1024,512]{0,1:T(8,128)(4,1)S(1)} %compare_and_fusion.2, f32[4,1024]{1,0:T(4,128)S(1)} %get-tuple-element.243, pred[]{:T(512)S(6)} %compare.11, ...), kind=kOutput, calls=%fused_computation.21.clone.1 | convolution fusion | flops 548929536 | bytes 13664257 | tf_op jit(solution)/shard_map/while/body/eval_jaxpr/hqk,khd->hqd/dot_general | solution.py:132
  322.8 4.9 fusion.79
  327.7 4.7 fusion.80
  333.5 5.8 %fusion.82 = f32[4,1024,128]{2,1,0:T(8,128)} fusion(f32[4,1024,128]{2,1,0:T(8,128)} %get-tuple-element.260, f32[4,512,1024]{2,1,0:T(8,128)S(1)} %copy-done.3, f32[4,1024]{1,0:T(4,128)S(1)} %select_maximum_fusion.2, pred[1024,512]{0,1:T(8,128)(4,1)S(1)} %compare_and_fusion.2, f32[4,1024]{1,0:T(4,128)S(1)} %get-tuple-element.243, pred[]{:T(512)S(6)} %compare.11, ...), kind=kOutput, calls=%fused_computation.21.clone.1 | convolution fusion | flops 548929536 | bytes 13664257 | tf_op jit(solution)/shard_map/while/body/eval_jaxpr/hqk,khd->hqd/dot_general | solution.py:132
  342.6 4.9 fusion.79
  347.5 4.7 fusion.80
  353.3 5.8 %fusion.82 = f32[4,1024,128]{2,1,0:T(8,128)} fusion(f32[4,1024,128]{2,1,0:T(8,128)} %get-tuple-element.260, f32[4,512,1024]{2,1,0:T(8,128)S(1)} %copy-done.3, f32[4,1024]{1,0:T(4,128)S(1)} %select_maximum_fusion.2, pred[1024,512]{0,1:T(8,128)(4,1)S(1)} %compare_and_fusion.2, f32[4,1024]{1,0:T(4,128)S(1)} %get-tuple-element.243, pred[]{:T(512)S(6)} %compare.11, ...), kind=kOutput, calls=%fused_computation.21.clone.1 | convolution fusion | flops 548929536 | bytes 13664257 | tf_op jit(solution)/shard_map/while/body/eval_jaxpr/hqk,khd->hqd/dot_general | solution.py:132
  362.4 4.9 fusion.79
  367.3 4.7 fusion.80
  373.1 5.8 %fusion.82 = f32[4,1024,128]{2,1,0:T(8,128)} fusion(f32[4,1024,128]{2,1,0:T(8,128)} %get-tuple-element.260, f32[4,512,1024]{2,1,0:T(8,128)S(1)} %copy-done.3, f32[4,1024]{1,0:T(4,128)S(1)} %select_maximum_fusion.2, pred[1024,512]{0,1:T(8,128)(4,1)S(1)} %compare_and_fusion.2, f32[4,1024]{1,0:T(4,128)S(1)} %get-tuple-element.243, pred[]{:T(512)S(6)} %compare.11, ...), kind=kOutput, calls=%fused_computation.21.clone.1 | convolution fusion | flops 548929536 | bytes 13664257 | tf_op jit(solution)/shard_map/while/body/eval_jaxpr/hqk,khd->hqd/dot_general | solution.py:132
  380.8 7.5 %gather_fusion.3 = bf16[2048,512]{1,0:T(8,128)(2,1)S(1)} fusion(bf16[1024,512]{1,0:T(8,128)(2,1)S(1)} %copy_bitcast_fusion.4, s32[2048]{0:T(1024)S(1)} %get-tuple-element.171), kind=kCustom, calls=%fused_computation.3 | custom fusion | bytes 4202496 | tf_op jit(solution)/shard_map/gather | solution.py:147
  388.4 14.1 %fusion.28 = f32[8,256,2048]{2,1,0:T(8,128)} fusion(bf16[8,512,2048]{2,1,0:T(8,128)(2,1)} %all-gather.11.cloned.1.call-done, bf16[8,256,512]{2,1,0:T(8,128)(2,1)S(1)} %bitcast.95, bf16[8,256]{1,0:T(8,128)(2,1)S(1)} %mul.110), kind=kOutput, calls=%fused_computation.55 | convolution fusion | flops 4296015872 | bytes 35655680 | tf_op jit(solution)/shard_map/ech,ehn->ecn/dot_general | solution.py:152
  402.5 11.6 %bitcast_multiply_fusion = f32[2048,2048]{1,0:T(8,128)} fusion(f32[8,256,2048]{2,1,0:T(8,128)} %fusion.28, f32[2048]{0:T(1024)S(1)} %scatter_custom_fusion.2), kind=kLoop, calls=%fused_computation.44 | loop fusion | flops 4194304 | bytes 33562624 | tf_op jit(solution)/shard_map/mul | solution.py:156
  414.2 29.3 %scatter_custom_fusion.3 = f32[512,2048]{1,0:T(8,128)} fusion(s32[2048]{0:T(1024)S(1)} %get-tuple-element.164, f32[2048,2048]{1,0:T(8,128)} %bitcast_multiply_fusion, f32[]{:T(128)} %constant.102.clone.1), kind=kCustom, calls=%fused_computation.58 | custom fusion | flops 4194304 | bytes 4194816 | tf_op jit(solution)/shard_map/scatter-add | solution.py:156
  443.4 3.9 convert_element_type.50
  449.9 3.3 all-to-all-start
  457.7 3.6 all-to-all-start.1
  461.4 15.2 %all-to-all-done.1 = bf16[8,4,16,2,512]{4,2,3,1,0:T(8,128)(2,1)S(1)} async-done(((bf16[8,4,16,2,512]{4,2,3,1,0:T(8,128)(2,1)}), bf16[8,4,16,2,512]{4,2,3,1,0:T(8,128)(2,1)S(1)}, u32[]{:S(2)}, u32[]{:S(2)}) %all-to-all-start.1) | async-done | bytes 1048608 | tf_op jit(solution)/shard_map/all_to_all | solution.py:48
  480.4 10.9 %reduce-scatter.2.cloned.1.call-done = bf16[512,512]{1,0:T(8,128)(2,1)} async-done(((bf16[512,2048]{1,0:T(8,128)(2,1)}), bf16[512,512]{1,0:T(8,128)(2,1)}) %reduce-scatter.2.cloned.1.call-update) | async-done | bytes 524304 | tf_op jit(solution)/shard_map/reduce_scatter | solution.py:158
  (161 shorter events, 64.3 us)
Async XLA Ops:
  7.2 82.1 %copy-start = (f32[2048,8]{0,1:T(8,128)S(1)}, f32[2048,8]{0,1:T(8,128)}, u32[]{:S(2)}) copy-start(f32[2048,8]{0,1:T(8,128)} %param.15) | copy-start | bytes 196612
  7.2 42.2 %all-gather.5.cloned.1.call-start = ((), (), s32[]{:S(2)}) async-start(), calls=%async_computation.3 | async-start | bytes 4718592 | tf_op jit(solution)/shard_map/all_gather | solution.py:90
  7.9 101.5 %all-gather.7.cloned.1.call-start = ((), (), s32[]{:S(2)}) async-start(), calls=%async_computation.4 | async-start | bytes 9437184 | tf_op jit(solution)/shard_map/all_gather | solution.py:112
  54.9 1.4 copy-start.6
  54.9 146.5 %all-gather.9.cloned.1.call-start = ((), (), s32[]{:S(2)}) async-start(), calls=%async_computation.5 | async-start | bytes 18874368 | tf_op jit(solution)/shard_map/all_gather | solution.py:89
  55.6 332.8 %all-gather.11.cloned.1.call-start = ((), (), s32[]{:S(2)}) async-start(), calls=%async_computation.6 | async-start | bytes 18874368 | tf_op jit(solution)/shard_map/all_gather | solution.py:150
  56.2 435.1 %reduce-scatter.2.cloned.1.call-start = ((), (), s32[]{:S(2)}) async-start(), calls=%async_computation.7 | async-start | bytes 2621440 | tf_op jit(solution)/shard_map/reduce_scatter | solution.py:158
  64.4 18.6 %copy-start.2 = (s32[4096]{0:T(1024)S(1)}, s32[4096]{0:T(1024)}, u32[]{:S(2)}) copy-start(s32[4096]{0:T(1024)} %param.12) | copy-start | bytes 49156
  226.5 5.8 %copy-start.3 = (f32[4,512,1024]{2,1,0:T(8,128)S(1)}, f32[4,512,1024]{2,1,0:T(8,128)}, u32[]{:S(2)}) copy-start(f32[4,512,1024]{2,1,0:T(8,128)} %get-tuple-element.241) | copy-start | bytes 25165828 | tf_op jit(solution)/shard_map/while
  246.5 6.5 %copy-start.3 = (f32[4,512,1024]{2,1,0:T(8,128)S(1)}, f32[4,512,1024]{2,1,0:T(8,128)}, u32[]{:S(2)}) copy-start(f32[4,512,1024]{2,1,0:T(8,128)} %get-tuple-element.241) | copy-start | bytes 25165828 | tf_op jit(solution)/shard_map/while
  267.0 6.2 %copy-start.3 = (f32[4,512,1024]{2,1,0:T(8,128)S(1)}, f32[4,512,1024]{2,1,0:T(8,128)}, u32[]{:S(2)}) copy-start(f32[4,512,1024]{2,1,0:T(8,128)} %get-tuple-element.241) | copy-start | bytes 25165828 | tf_op jit(solution)/shard_map/while
  287.1 6.9 %copy-start.3 = (f32[4,512,1024]{2,1,0:T(8,128)S(1)}, f32[4,512,1024]{2,1,0:T(8,128)}, u32[]{:S(2)}) copy-start(f32[4,512,1024]{2,1,0:T(8,128)} %get-tuple-element.241) | copy-start | bytes 25165828 | tf_op jit(solution)/shard_map/while
  307.9 5.8 %copy-start.3 = (f32[4,512,1024]{2,1,0:T(8,128)S(1)}, f32[4,512,1024]{2,1,0:T(8,128)}, u32[]{:S(2)}) copy-start(f32[4,512,1024]{2,1,0:T(8,128)} %get-tuple-element.241) | copy-start | bytes 25165828 | tf_op jit(solution)/shard_map/while
  327.7 5.8 %copy-start.3 = (f32[4,512,1024]{2,1,0:T(8,128)S(1)}, f32[4,512,1024]{2,1,0:T(8,128)}, u32[]{:S(2)}) copy-start(f32[4,512,1024]{2,1,0:T(8,128)} %get-tuple-element.241) | copy-start | bytes 25165828 | tf_op jit(solution)/shard_map/while
  347.5 5.8 %copy-start.3 = (f32[4,512,1024]{2,1,0:T(8,128)S(1)}, f32[4,512,1024]{2,1,0:T(8,128)}, u32[]{:S(2)}) copy-start(f32[4,512,1024]{2,1,0:T(8,128)} %get-tuple-element.241) | copy-start | bytes 25165828 | tf_op jit(solution)/shard_map/while
  367.3 5.8 %copy-start.3 = (f32[4,512,1024]{2,1,0:T(8,128)S(1)}, f32[4,512,1024]{2,1,0:T(8,128)}, u32[]{:S(2)}) copy-start(f32[4,512,1024]{2,1,0:T(8,128)} %get-tuple-element.241) | copy-start | bytes 25165828 | tf_op jit(solution)/shard_map/while
  443.4 4.0 copy-start.4
  443.4 9.7 %copy-start.5 = (bf16[512,2,512]{2,0,1:T(8,128)(2,1)S(1)}, bf16[512,2,512]{2,0,1:T(8,128)(2,1)}, u32[]{:S(2)}) copy-start(bf16[512,2,512]{2,0,1:T(8,128)(2,1)} %fusion.35) | copy-start | bytes 3145732
  449.9 7.8 %all-to-all-start = ((s32[8,1,4]{2,1,0:T(1,128)}), s32[8,1,4]{2,1,0:T(1,128)S(1)}, u32[]{:S(2)}, u32[]{:S(2)}) async-start(s32[8,1,4]{2,1,0:T(1,128)} %bitcast.11), calls=%async_computation.1 | async-start | bytes 8192 | tf_op jit(solution)/shard_map/all_to_all | solution.py:49
  457.7 18.9 %all-to-all-start.1 = ((bf16[8,4,16,2,512]{4,2,3,1,0:T(8,128)(2,1)}), bf16[8,4,16,2,512]{4,2,3,1,0:T(8,128)(2,1)S(1)}, u32[]{:S(2)}, u32[]{:S(2)}) async-start(bf16[8,4,16,2,512]{4,2,3,1,0:T(8,128)(2,1)} %bitcast.14), calls=%async_computation.2 | async-start | bytes 2097152 | tf_op jit(solution)/shard_map/all_to_all | solution.py:48
  461.3 32.2 %copy-start.1 = (f32[2048,8]{0,1:T(8,128)S(1)}, f32[2048,8]{0,1:T(8,128)}, u32[]{:S(2)}) copy-start(f32[2048,8]{0,1:T(8,128)} %param.15) | copy-start | bytes 196612
Sparse Core Ops, SparseCore 0:
  9.9 39.4 all-gather.4
  55.0 54.3 all-gather.6
  111.4 89.9 all-gather.8
  203.1 93.1 all-gather.10
  447.5 43.7 reduce-scatter.1
where the time goes:
time: 501 us; the launch traced here: 500 us
  waiting for transfers between devices  154 us (31%)
  matrix products  119 us (24%)
  other arithmetic  103 us (21%)
  local copies, waits for them, and re-layouts  102 us (20%)
  between operations  14.2 us (3%)
  starting transfers between devices  7.07 us (1%)
    all_gather x1, waiting for transfers between devices, local(): query_part = lax.all_gather(query_weight, 'tok', axis=1, tiled=True)  72.1 us
    dot_general x8, matrix products, one_block(): jnp.einsum('hqk,khd->hqd', expon.astype(jnp.bfloat16), value_block, prefe...  44.8 us
    dot_general x8, matrix products, one_block(): jnp.einsum('hqd,khd->hqk', by_head_q, key_block, preferred_element_type=j...  40.6 us
    reduce_sum x8, other arithmetic, one_block(): total = total * shrink + jnp.sum(expon, axis=-1)  38 us
    all_gather x1, waiting for transfers between devices, local(): key_part = lax.all_gather(kv_weight, 'tok', axis=1, tiled=True)  37.2 us
    scatter-add x1, other arithmetic, local(): jnp.zeros((tok_dev, count), jnp.float32).at[slot_token]  29.3 us
    dynamic_slice x16, local copies, waits for them, and re-layouts, local(): state, _ = lax.scan(one_block, state, (key_blocks, value_blocks, firsts))  17.4 us
    all_to_all x1, waiting for transfers between devices, place_pages(): lax.all_to_all(outgoing, 'tok', split_axis=0, concat_axis=0, tiled=True)  15.2 us
  transfers between devices with their start and end apart: 7, of which 6 were waited for; matrix products, arithmetic and copies ran while one was open for 49% of the time, Pallas kernels for 0%

commit v1 on v0

v1 whole, which is shorter than its diff:
```python
import functools
import math

import jax
import jax.numpy as jnp
from jax import lax
from jax.experimental import pallas as pl
from jax.experimental.pallas import tpu as pltpu
from jax.sharding import PartitionSpec as P

HDIM = 128
SEGS = 4
EPSILON = 1e-05
MASKED = -1e30
VMEM_BYTES = 48 * 1024 * 1024
SCALE = math.log2(math.e) / math.sqrt(HDIM)


def rms_norm(hidden, norm_gain):
    values = hidden.astype(jnp.float32)
    factor = lax.rsqrt(jnp.mean(values * values, axis=-1, keepdims=True) + EPSILON)
    return (values * factor * norm_gain).astype(jnp.bfloat16)


def route_gates(normed, router_weight, routes):
    logits = jnp.dot(normed.astype(jnp.float32), router_weight, precision=lax.Precision.HIGHEST)
    expert_ids = jnp.arange(logits.shape[1], dtype=jnp.int32)
    picked = routes[:, :, None] == expert_ids[None, None, :]
    chosen = jnp.sum(jnp.where(picked, logits[:, None, :], jnp.float32(0.0)), axis=-1)
    gates = jax.nn.softmax(chosen, axis=-1)
    return jnp.sum(jnp.where(picked, gates[:, :, None], jnp.float32(0.0)), axis=1)


def params():
    return pltpu.CompilerParams(
        dimension_semantics=("arbitrary",), vmem_limit_bytes=VMEM_BYTES
    )


def kv_kernel(x_ref, w_ref, out_ref):
    depth = w_ref.shape[0] * w_ref.shape[2]
    w = w_ref[:, 0].reshape(depth, w_ref.shape[3])
    out_ref[0] = jnp.dot(x_ref[...], w, preferred_element_type=jnp.float32).astype(jnp.bfloat16)


def project_kv(normed, weight):
    shards, kinds, rows, cols = weight.shape
    tokens, width = normed.shape
    return pl.pallas_call(
        kv_kernel,
        grid=(kinds,),
        in_specs=[
            pl.BlockSpec((tokens, width), lambda c: (0, 0)),
            pl.BlockSpec((shards, 1, rows, cols), lambda c: (0, c, 0, 0)),
        ],
        out_specs=pl.BlockSpec((1, tokens, cols), lambda c: (c, 0, 0)),
        out_shape=jax.ShapeDtypeStruct((kinds, tokens, cols), jnp.bfloat16),
        compiler_params=params(),
        cost_estimate=pl.CostEstimate(
            flops=2 * kinds * tokens * width * cols,
            bytes_accessed=2 * (weight.size + normed.size + kinds * tokens * cols),
            transcendentals=0,
        ),
        name="project_kv",
    )(normed, weight)


def query_kernel(x_ref, routes_ref, w_ref, out_ref):
    expert = pl.program_id(0)
    depth = w_ref.shape[0] * w_ref.shape[2]
    w = w_ref[:, 0].reshape(depth, w_ref.shape[3])
    y = jnp.dot(x_ref[...], w, preferred_element_type=jnp.float32).astype(jnp.bfloat16)

    @pl.when(expert == 0)
    def _():
        out_ref[...] = jnp.zeros_like(out_ref)

    for slot in range(out_ref.shape[0]):
        mine = routes_ref[:, slot : slot + 1] == expert
        out_ref[slot] = jnp.where(mine, y, out_ref[slot])


def project_queries(normed, routes, weight):
    shards, experts, rows, cols = weight.shape
    tokens, width = normed.shape
    slots = routes.shape[1]
    return pl.pallas_call(
        query_kernel,
        grid=(experts,),
        in_specs=[
            pl.BlockSpec((tokens, width), lambda e: (0, 0)),
            pl.BlockSpec((tokens, slots), lambda e: (0, 0)),
            pl.BlockSpec((shards, 1, rows, cols), lambda e: (0, e, 0, 0)),
        ],
        out_specs=pl.BlockSpec((slots, tokens, cols), lambda e: (0, 0, 0)),
        out_shape=jax.ShapeDtypeStruct((slots, tokens, cols), jnp.bfloat16),
        compiler_params=params(),
        cost_estimate=pl.CostEstimate(
            flops=2 * experts * tokens * width * cols,
            bytes_accessed=2 * (weight.size + normed.size + slots * tokens * cols),
            transcendentals=0,
        ),
        name="project_queries",
    )(normed, routes, weight)


def attention_kernel(bounds_ref, q_ref, lower_ref, kv_ref, out_ref, *, block_k, heads, tile):
    pos_first = bounds_ref[0]
    step = pl.program_id(1)
    first = pos_first + step * tile
    low = bounds_ref[1 + 2 * step]
    high = bounds_ref[2 + 2 * step]
    slots = q_ref.shape[0]
    columns = slots * tile
    per_shard = kv_ref.shape[2] // block_k
    begin = low // block_k
    end = (first + tile - 1) // block_k + 1
    q_pos = first + lax.broadcasted_iota(jnp.int32, (1, columns), 1) % tile
    lower = jnp.concatenate([lower_ref[0]] * slots, axis=1)
    queries = [
        q_ref[:, :, h * HDIM : (h + 1) * HDIM].reshape(columns, HDIM) for h in range(heads)
    ]

    def body(block, carry, masked):
        shard = block // per_shard
        rows = pl.ds((block % per_shard) * block_k, block_k)
        if masked:
            k_pos = block * block_k + lax.broadcasted_iota(jnp.int32, (block_k, columns), 0)
            allowed = (k_pos >= lower) & (k_pos <= q_pos)
        result = []
        for h in range(heads):
            peak, total, accum = carry[h]
            span = slice(h * HDIM, (h + 1) * HDIM)
            keys = kv_ref[shard, 0, rows, span]
            values = kv_ref[shard, 1, rows, span]
            scores = lax.dot_general(
                keys, queries[h], (((1,), (1,)), ((), ())), preferred_element_type=jnp.float32
            ) * SCALE
            if masked:
                scores = jnp.where(allowed, scores, MASKED)
            new_peak = jnp.maximum(peak, jnp.max(scores, axis=0, keepdims=True))
            expon = jnp.exp2(scores - new_peak)
            if masked:
                expon = jnp.where(allowed, expon, 0.0)
            shrink = jnp.exp2(peak - new_peak)
            total = total * shrink + jnp.sum(expon, axis=0, keepdims=True)
            accum = accum * shrink + lax.dot_general(
                values,
                expon.astype(jnp.bfloat16),
                (((0,), (0,)), ((), ())),
                preferred_element_type=jnp.float32,
            )
            result.append((new_peak, total, accum))
        return tuple(result)

    state = tuple(
        (
            jnp.full((1, columns), MASKED, jnp.float32),
            jnp.zeros((1, columns), jnp.float32),
            jnp.zeros((HDIM, columns), jnp.float32),
        )
        for _ in range(heads)
    )
    inner = jnp.maximum((first + 1) // block_k, begin)
    clear = jnp.clip((high + block_k - 1) // block_k, begin, inner)
    state = lax.fori_loop(begin, clear, functools.partial(body, masked=True), state)
    state = lax.fori_loop(clear, inner, functools.partial(body, masked=False), state)
    state = lax.fori_loop(inner, end, functools.partial(body, masked=True), state)
    for h in range(heads):
        _, total, accum = state[h]
        rows = (accum / total).T.astype(jnp.bfloat16)
        out_ref[:, :, h * HDIM : (h + 1) * HDIM] = rows.reshape(slots, tile, HDIM)


def attend(queries, lower, key_values, first):
    slots, tokens, cols = queries.shape
    shards, kinds, rows, _ = key_values.shape
    heads = math.gcd(cols // HDIM, 2)
    tile = math.gcd(tokens, 256)
    block_k = math.gcd(rows, 512)
    by_tile = lower.reshape(tokens // tile, tile)
    bounds = jnp.concatenate(
        [first[None], jnp.stack([by_tile[:, 0], by_tile[:, -1]], axis=1).reshape(-1)]
    ).astype(jnp.int32)
    return pl.pallas_call(
        functools.partial(attention_kernel, block_k=block_k, heads=heads, tile=tile),
        grid=(cols // (heads * HDIM), tokens // tile),
        in_specs=[
            pl.BlockSpec(memory_space=pltpu.SMEM),
            pl.BlockSpec((slots, tile, heads * HDIM), lambda g, t: (0, t, g)),
            pl.BlockSpec((1, 1, tile), lambda g, t: (t, 0, 0)),
            pl.BlockSpec((shards, kinds, rows, heads * HDIM), lambda g, t: (0, 0, 0, g)),
        ],
        out_specs=pl.BlockSpec((slots, tile, heads * HDIM), lambda g, t: (0, t, g)),
        out_shape=jax.ShapeDtypeStruct((slots, tokens, cols), jnp.bfloat16),
        compiler_params=pltpu.CompilerParams(
            dimension_semantics=("arbitrary", "arbitrary"), vmem_limit_bytes=VMEM_BYTES
        ),
        cost_estimate=pl.CostEstimate(
            flops=4 * slots * tokens * cols * 2048,
            bytes_accessed=2 * (queries.size * 2 + key_values.size),
            transcendentals=slots * tokens * (cols // HDIM) * 2048,
        ),
        name="attend",
    )(bounds, queries, by_tile[:, None, :], key_values)


def out_kernel(x_ref, routes_ref, gates_ref, w_ref, out_ref, picked):
    experts = w_ref.shape[1]

    @pl.when(pl.program_id(0) == 0)
    def _():
        for e in range(experts):
            rows = jnp.zeros_like(x_ref[0])
            for slot in range(x_ref.shape[0]):
                rows = jnp.where(routes_ref[:, slot : slot + 1] == e, x_ref[slot], rows)
            picked[e] = rows

    total = jnp.zeros(out_ref.shape[1:], jnp.float32)
    for e in range(experts):
        term = jnp.dot(picked[e], w_ref[0, e], preferred_element_type=jnp.float32)
        total = total + gates_ref[:, e : e + 1] * term
    out_ref[0] = total.astype(jnp.bfloat16)


def project_out(attended, routes, gates, weight, parts):
    shards, experts, rows, cols = weight.shape
    slots, tokens, _ = attended.shape
    span = shards * cols // parts
    per = span // cols
    return pl.pallas_call(
        out_kernel,
        grid=(shards,),
        in_specs=[
            pl.BlockSpec((slots, tokens, rows), lambda i: (0, 0, 0)),
            pl.BlockSpec((tokens, slots), lambda i: (0, 0)),
            pl.BlockSpec((tokens, experts), lambda i: (0, 0)),
            pl.BlockSpec((1, experts, rows, cols), lambda i: (i, 0, 0, 0)),
        ],
        out_specs=pl.BlockSpec((1, tokens, cols), lambda i: (i // per, 0, i % per)),
        out_shape=jax.ShapeDtypeStruct((parts, tokens, span), jnp.bfloat16),
        scratch_shapes=[pltpu.VMEM((experts, tokens, rows), jnp.bfloat16)],
        compiler_params=params(),
        cost_estimate=pl.CostEstimate(
            flops=2 * experts * tokens * rows * shards * cols,
            bytes_accessed=2 * (weight.size + attended.size + tokens * shards * cols),
            transcendentals=0,
        ),
        name="project_out",
    )(attended, routes, gates, weight)


def local(
    hidden,
    segment_ids,
    routes,
    norm_gain,
    router_weight,
    query_weight,
    kv_weight,
    out_weight,
    page_table,
):
    tok_dev, width = hidden.shape
    head_cols = query_weight.shape[2]
    shards = lax.axis_size("tok")
    parts = lax.axis_size("mdl")
    tok_row = lax.axis_index("tok")
    pages_here = page_table.shape[0]
    page_rows = tok_dev // pages_here

    kv_full = lax.all_gather(kv_weight, "tok", axis=0)
    table = lax.all_gather(page_table, "tok", axis=0, tiled=True)
    normed = rms_norm(hidden, norm_gain)
    gates = route_gates(normed, router_weight, routes)
    key_values = lax.all_gather(project_kv(normed, kv_full), "tok", axis=0)
    query_full = lax.all_gather(query_weight, "tok", axis=0)
    out_full = lax.all_gather(out_weight, "tok", axis=0)

    here = tok_row * pages_here + jnp.arange(pages_here, dtype=jnp.int32)
    logical = jnp.arange(table.shape[0], dtype=jnp.int32)
    source = jnp.sum(jnp.where(table[None, :] == here[:, None], logical[None, :], 0), axis=1)
    paged = key_values.reshape(shards, 2, pages_here, page_rows, head_cols)
    cache = paged[source // pages_here, :, source % pages_here].transpose(0, 2, 1, 3)

    prompt_ids = jnp.arange(SEGS, dtype=jnp.int32)
    seg_first = jnp.sum((segment_ids[:, None] < prompt_ids[None, :]).astype(jnp.int32), axis=0)
    first = (tok_row * tok_dev).astype(jnp.int32)
    own_seg = lax.dynamic_slice_in_dim(segment_ids, first, tok_dev, 0)
    lower = jnp.sum(
        jnp.where(own_seg[:, None] == prompt_ids[None, :], seg_first[None, :], 0), axis=1
    )

    queries = project_queries(normed, routes, query_full)
    attended = attend(queries, lower, key_values, first)
    partial_sums = project_out(attended, routes, gates, out_full, parts)
    mine = lax.psum_scatter(partial_sums, "mdl", scatter_dimension=0, tiled=False)
    span = width // parts
    residual = lax.dynamic_slice_in_dim(hidden, lax.axis_index("mdl") * span, span, 1)
    output = (residual.astype(jnp.float32) + mine.astype(jnp.float32)).astype(jnp.bfloat16)
    return (output, cache)


def solution(mesh):
    placed = (
        P("tok", None),
        P(),
        P("tok", None),
        P(),
        P(),
        P(None, "tok", "mdl"),
        P(None, "tok", "mdl"),
        P(None, "mdl", "tok"),
        P("tok"),
    )
    return jax.shard_map(
        local,
        mesh=mesh,
        in_specs=placed,
        out_specs=(P("tok", "mdl"), P("tok", None, None, "mdl")),
        check_vma=False,
    )
```

time: 501 us -> 358 us (0.71)
  waiting for transfers between devices: 154 us -> 272 us
  matrix products: 119 us -> 1.72 us
  other arithmetic: 103 us -> 7.04 us
  local copies, waits for them, and re-layouts: 102 us -> 9.64 us
  Pallas kernels: 0 us -> 45 us
  blocking collectives: 0 us -> 7.02 us
  starting transfers between devices: 7.07 us -> 0.19 us
    all_gather x4, waiting for transfers between devices: 123 us -> 241 us  [the longest x1 83.4 us: local(): query_full = lax.all_gather(query_weight, 'tok', axis=0)]
    dot_general x19 -> x0, matrix products: 118 us -> none  [the longest x8 44.8 us: one_block(): jnp.einsum('hqk,khd->hqd', expon.astype(jnp.bfloat16), value_block, prefe...]
    pallas_call x0 -> x4, Pallas kernels: none -> 45 us  [the longest x1 15.6 us: project_out(): pl.pallas_call(out_kernel, grid=(shards,), in_specs=[pl.BlockSpec((slots,...]
    reduce_sum x12 -> x4, other arithmetic: 38.3 us -> 0.3 us  [the longest x1 0.18 us: local(): jnp.sum(jnp.where(table[None, :] == here[:, None], logical[None, :], 0),...]
    scatter-add x1 -> x0, other arithmetic: 29.3 us -> none  [local(): jnp.zeros((tok_dev, count), jnp.float32).at[slot_token]]
    gather x6 -> x1, local copies, waits for them, and re-layouts: 30.9 us -> 4.01 us  [local(): paged[source // pages_here, :, source % pages_here].transpose(0, 2, 1, 3)]
    scatter x5 -> x0, local copies, waits for them, and re-layouts: 18.7 us -> none  [the longest x1 7.58 us: local(): jnp.zeros((experts * capacity,), jnp.bfloat16).at[slots]]
    reduce_scatter x1, waiting for transfers between devices: 10.9 us -> 29.2 us  [local(): lax.psum_scatter(partial_sums, 'mdl', scatter_dimension=0, tiled=False)]
  transfers between devices with their start and end apart: 7 -> 5, of which waited for: 6 -> 5; matrix products, arithmetic and copies ran while one was open for 49% -> 4% of each run, Pallas kernels for 0% -> 8%
where the time goes in v1:
time: 358 us; the launch traced here: 357 us
  waiting for transfers between devices  272 us (76%)
  Pallas kernels  45 us (13%)
  between operations  14.6 us (4%)
  local copies, waits for them, and re-layouts  9.64 us (3%)
  other arithmetic  7.04 us (2%)
  blocking collectives  7.02 us (2%)
    all_gather x1, waiting for transfers between devices, local(): query_full = lax.all_gather(query_weight, 'tok', axis=0)  83.4 us
    all_gather x1, waiting for transfers between devices, local(): out_full = lax.all_gather(out_weight, 'tok', axis=0)  80.2 us
    all_gather x1, waiting for transfers between devices, local(): key_values = lax.all_gather(project_kv(normed, kv_full), 'tok', axis=0)  41.1 us
    all_gather x1, waiting for transfers between devices, local(): kv_full = lax.all_gather(kv_weight, 'tok', axis=0)  36.4 us
    reduce_scatter x1, waiting for transfers between devices, local(): lax.psum_scatter(partial_sums, 'mdl', scatter_dimension=0, tiled=False)  29.2 us
    pallas_call x1, Pallas kernels, project_out(): pl.pallas_call(out_kernel, grid=(shards,), in_specs=[pl.BlockSpec((slots,...  15.6 us
    pallas_call x1, Pallas kernels, project_queries(): pl.pallas_call(query_kernel, grid=(experts,), in_specs=[pl.BlockSpec((tok...  14.2 us
    pallas_call x1, Pallas kernels, attend(): pl.pallas_call(functools.partial(attention_kernel, block_k=block_k, heads...  10.2 us
  transfers between devices with their start and end apart: 5, of which 5 were waited for; matrix products, arithmetic and copies ran while one was open for 4% of the time, Pallas kernels for 8%

profile of v1, /device:TPU:0, one launch (start us, length us, event | category | flops | bytes accessed | tf_op | source)
XLA Modules:
  0.0 357.4 jit_solution(9609055856954141275)
XLA Ops:
  7.2 0.0 copy-start
  7.2 0.0 copy-start.5
  7.2 0.0 all-gather.11.cloned.1.call-start
  7.2 0.7 all-gather.11.cloned.1.call-update
  7.9 0.0 all-gather.9.cloned.1.call-start
  8.0 0.7 all-gather.9.cloned.1.call-update
  8.7 0.0 all-gather.13.cloned.1.call-start
  8.7 2.1 fusion
  10.8 0.0 copy-done.5
  10.8 2.1 fusion.2.x_ref
  13.0 36.4 %all-gather.11.cloned.1.call-done = bf16[16,256,512]{2,1,0:T(8,128)(2,1)} async-done(((bf16[2,256,512]{2,1,0:T(8,128)(2,1)}), bf16[16,256,512]{2,1,0:T(8,128)(2,1)}) %all-gather.11.cloned.1.call-update) | async-done | bytes 4194320 | tf_op jit(solution)/shard_map/all_gather | solution.py:272
  49.4 4.9 %project_kv.1 = bf16[2,512,512]{2,1,0:T(8,128)(2,1)} custom-call(bf16[512,2048]{1,0:T(8,128)(2,1)S(1)} %fusion.2.x_ref, bf16[8,2,256,512]{3,2,1,0:T(8,128)(2,1)} %bitcast.37), custom_call_target="tpu_custom_call" | custom-call | flops 2147483648 | bytes 7340032 | tf_op jit(solution)/shard_map/project_kv/pallas_call | solution.py:49
  54.3 0.0 all-gather.13.cloned.1.call-update
  54.3 0.0 all-gather.15.cloned.1.call-start
  54.4 0.5 all-gather.15.cloned.1.call-update
  54.9 0.0 reduce-scatter.2.cloned.1.call-start
  54.9 0.0 copy-done.4
  55.0 0.1 dynamic_slice.7
  55.0 0.1 convert_reduce_fusion
  55.2 0.1 select_reduce_fusion.3
  55.3 0.1 fusion.12
  55.4 0.1 pad_add_fusion
  55.4 0.1 reshape.160
  55.5 0.0 copy-done.3
  55.5 0.2 copy.25.routes_ref
  55.7 0.0 copy-done
  55.7 1.7 fusion.13
  57.5 0.1 copy.27.gates_ref
  57.7 0.1 pad_add_fusion.1.bounds_ref
  57.8 83.4 %all-gather.9.cloned.1.call-done = bf16[64,256,512]{2,1,0:T(8,128)(2,1)} async-done(((bf16[8,256,512]{2,1,0:T(8,128)(2,1)}), bf16[64,256,512]{2,1,0:T(8,128)(2,1)}) %all-gather.9.cloned.1.call-update) | async-done | bytes 16777232 | tf_op jit(solution)/shard_map/all_gather | solution.py:277
  141.1 14.2 %project_queries.1.q_ref = bf16[2,512,512]{2,1,0:T(8,128)(2,1)S(1)} custom-call(bf16[512,2048]{1,0:T(8,128)(2,1)S(1)} %fusion.2.x_ref, s32[512,2]{1,0:T(8,128)S(1)} %copy.25.routes_ref, bf16[8,8,256,512]{3,2,1,0:T(8,128)(2,1)} %bitcast.35), custom_call_target="tpu_custom_call" | custom-call | flops 8589934592 | bytes 19922944 | tf_op jit(solution)/shard_map/project_queries/pallas_call | solution.py:87
  155.4 0.0 copy-start.1
  155.4 1.0 copy-done.1
  156.3 41.1 %all-gather.13.cloned.1.call-done = bf16[16,512,512]{2,1,0:T(8,128)(2,1)} async-done(((bf16[2,512,512]{2,1,0:T(8,128)(2,1)}), bf16[16,512,512]{2,1,0:T(8,128)(2,1)}) %all-gather.13.cloned.1.call-update) | async-done | bytes 8388624 | tf_op jit(solution)/shard_map/all_gather | solution.py:276
  197.5 1.2 copy-done.2
  198.7 10.2 %attend.1.x_ref = bf16[2,512,512]{2,1,0:T(8,128)(2,1)S(1)} custom-call(s32[5]{0:T(128)S(1)} %pad_add_fusion.1.bounds_ref, bf16[2,512,512]{2,1,0:T(8,128)(2,1)S(1)} %copy-done.2, s32[2,1,256]{2,1,0:T(1,128)S(1)} %bitcast.31, bf16[8,2,512,512]{3,2,1,0:T(8,128)(2,1)} %bitcast.33), custom_call_target="tpu_custom_call" | custom-call | flops 4294967296 | bytes 10485760 | tf_op jit(solution)/shard_map/attend/pallas_call | solution.py:185
  208.9 80.2 %all-gather.15.cloned.1.call-done = bf16[64,512,256]{2,1,0:T(8,128)(2,1)} async-done(((bf16[8,512,256]{2,1,0:T(8,128)(2,1)}), bf16[64,512,256]{2,1,0:T(8,128)(2,1)}) %all-gather.15.cloned.1.call-update) | async-done | bytes 16777232 | tf_op jit(solution)/shard_map/all_gather | solution.py:278
  289.1 15.6 %project_out.1 = bf16[4,512,512]{2,1,0:T(8,128)(2,1)} custom-call(bf16[2,512,512]{2,1,0:T(8,128)(2,1)S(1)} %attend.1.x_ref, s32[512,2]{1,0:T(8,128)S(1)} %copy.25.routes_ref, f32[512,8]{1,0:T(8,128)S(1)} %copy.27.gates_ref, bf16[8,8,512,256]{3,2,1,0:T(8,128)(2,1)} %bitcast.36), custom_call_target="tpu_custom_call" | custom-call | flops 8589934592 | bytes 19922944 | tf_op jit(solution)/shard_map/project_out/pallas_call | solution.py:231
  304.7 0.0 reduce-scatter.2.cloned.1.call-update
  304.7 0.0 copy-done.7
  304.7 0.6 dynamic-slice
  306.0 0.2 dynamic-update-slice
  306.2 7.0 %all-reduce = s32[256]{0:T(256)S(1)} all-reduce(s32[256]{0:T(256)S(1)} %dynamic-update-slice), channel_id=1, replica_groups=mesh['tok'=8,'mdl'=4] {'tok'}, use_global_device_ids=true, to_apply=%add | all-reduce | flops 256 | bytes 2048
  313.3 0.2 select_reduce_fusion
  313.5 4.0 %gather_fusion = bf16[32,2,16,512]{3,2,1,0:T(8,128)(2,1)S(1)} fusion(bf16[8,2,32,16,512]{4,3,2,1,0:T(8,128)(2,1)} %bitcast.34, s32[32]{0:T(128)S(1)} %fusion.11), kind=kCustom, calls=%fused_computation | custom fusion | bytes 2097408 | tf_op jit(solution)/shard_map/gather | solution.py:284
  317.5 2.1 copy.28
  319.5 29.2 %reduce-scatter.2.cloned.1.call-done = bf16[1,512,512]{2,1,0:T(8,128)(2,1)} async-done(((bf16[4,512,512]{2,1,0:T(8,128)(2,1)}), bf16[1,512,512]{2,1,0:T(8,128)(2,1)}) %reduce-scatter.2.cloned.1.call-update) | async-done | bytes 524304 | tf_op jit(solution)/shard_map/reduce_scatter | solution.py:297
  348.7 2.1 fusion.3
  (16 shorter events, 0.2 us)
Async XLA Ops:
  7.2 48.5 %copy-start = (f32[2048,8]{0,1:T(8,128)S(1)}, f32[2048,8]{0,1:T(8,128)}, u32[]{:S(2)}) copy-start(f32[2048,8]{0,1:T(8,128)} %param.13) | copy-start | bytes 196612
  7.2 3.6 %copy-start.5 = (f32[2048]{0:T(1024)S(1)}, f32[2048]{0:T(1024)}, u32[]{:S(2)}) copy-start(f32[2048]{0:T(1024)} %param.12) | copy-start | bytes 24580
  7.2 42.2 %all-gather.11.cloned.1.call-start = ((), (), s32[]{:S(2)}) async-start(), calls=%async_computation.3 | async-start | bytes 4718592 | tf_op jit(solution)/shard_map/all_gather | solution.py:272
  7.9 133.2 %all-gather.9.cloned.1.call-start = ((), (), s32[]{:S(2)}) async-start(), calls=%async_computation.2 | async-start | bytes 18874368 | tf_op jit(solution)/shard_map/all_gather | solution.py:277
  8.7 188.8 %all-gather.13.cloned.1.call-start = ((), (), s32[]{:S(2)}) async-start(), calls=%async_computation.4 | async-start | bytes 9437184 | tf_op jit(solution)/shard_map/all_gather | solution.py:276
  49.4 5.6 %copy-start.4 = (s32[4096]{0:T(1024)S(1)}, s32[4096]{0:T(1024)}, u32[]{:S(2)}) copy-start(s32[4096]{0:T(1024)} %param.10) | copy-start | bytes 49156
  49.4 6.2 %copy-start.3 = (s32[512,2]{0,1:T(2,128)S(1)}, s32[512,2]{0,1:T(2,128)}, u32[]{:S(2)}) copy-start(s32[512,2]{0,1:T(2,128)} %param.11) | copy-start | bytes 12292
  54.3 234.8 %all-gather.15.cloned.1.call-start = ((), (), s32[]{:S(2)}) async-start(), calls=%async_computation.5 | async-start | bytes 18874368 | tf_op jit(solution)/shard_map/all_gather | solution.py:278
  54.9 293.8 %reduce-scatter.2.cloned.1.call-start = ((), (), s32[]{:S(2)}) async-start(), calls=%async_computation.1 | async-start | bytes 2621440 | tf_op jit(solution)/shard_map/reduce_scatter | solution.py:297
  155.4 1.0 copy-start.1
  197.5 1.2 copy-start.2
  289.1 15.6 %copy-start.7 = (u32[32]{0:T(128)S(1)}, u32[32]{0:T(128)}, u32[]{:S(2)}) copy-start(u32[32]{0:T(128)} %constant.73) | copy-start | bytes 388
  289.1 16.9 %copy-start.6 = (s32[32]{0:T(128)S(1)}, s32[32]{0:T(128)}, u32[]{:S(2)}) copy-start(s32[32]{0:T(128)} %param.17) | copy-start | bytes 388
Sparse Core Ops, SparseCore 0:
  9.9 39.4 all-gather.10
  51.2 89.8 all-gather.8
  143.0 54.3 all-gather.12
  199.2 89.8 all-gather.14
  304.8 43.8 reduce-scatter.1

commit v2 on v1

--- a/solution.py
+++ b/solution.py
@@ -250,6 +250,296 @@
     )(attended, routes, gates, weight)
 
 
+def gather_kernel(
+    x_ref,
+    routes_ref,
+    kvw_ref,
+    qw_ref,
+    q_ref,
+    gathered_ref,
+    weights,
+    own_kv,
+    send_sem,
+    recv_sem,
+    local_sem,
+):
+    me = lax.axis_index("tok")
+    core, col, row = me % 2, (me // 2) % 2, me // 4
+    to_core, to_col, to_row = 1 - 2 * core, 2 - 4 * col, 4 - 8 * row
+    mate, side, over = me + to_core, me + to_col, me + to_row
+    across = me + to_col + to_row
+
+    barrier = pltpu.get_barrier_semaphore()
+    for other in (mate, side, over):
+        pl.semaphore_signal(
+            barrier, inc=1, device_id={"tok": other}, device_id_type=pl.DeviceIdType.MESH
+        )
+    pl.semaphore_wait(barrier, 3)
+
+    kinds, experts = kvw_ref.shape[0], qw_ref.shape[0]
+    early = min(2, experts)
+    order = [("w", c) for c in range(kinds + early)]
+    order += [("kv", c) for c in range(kinds)]
+    order += [("w", c) for c in range(kinds + early, kinds + experts)]
+    count = len(order)
+
+    def source(chunk):
+        kind, c = chunk
+        if kind == "kv":
+            return own_kv.at[c]
+        return kvw_ref.at[c] if c < kinds else qw_ref.at[c - kinds]
+
+    def slot(chunk, shard):
+        kind, c = chunk
+        return gathered_ref.at[shard, c] if kind == "kv" else weights.at[c, shard]
+
+    def half(ref, part):
+        rows = ref.shape[0] // 2
+        return ref.at[pl.ds(part * rows, rows)]
+
+    def copy(k, way, src, dst, other):
+        return pltpu.make_async_remote_copy(
+            src_ref=src,
+            dst_ref=dst,
+            send_sem=send_sem.at[k, way],
+            recv_sem=recv_sem.at[k, way],
+            device_id={"tok": other},
+            device_id_type=pl.DeviceIdType.MESH,
+        )
+
+    def send(k, way):
+        chunk = order[k]
+        if way < 3:
+            return copy(k, way, source(chunk), slot(chunk, me), (mate, side, over)[way])
+        place, other = [
+            (half(slot(chunk, over), 0), side),
+            (half(slot(chunk, side), 1), over),
+            (slot(chunk, side), mate),
+            (slot(chunk, over), mate),
+            (slot(chunk, across), mate),
+        ][way - 3]
+        return copy(k, way, place, place, other)
+
+    def arrival(k, way):
+        chunk = order[k]
+        place = [
+            slot(chunk, mate),
+            slot(chunk, side),
+            slot(chunk, over),
+            half(slot(chunk, across), 0),
+            half(slot(chunk, across), 1),
+            slot(chunk, side + to_core),
+            slot(chunk, over + to_core),
+            slot(chunk, across + to_core),
+        ][way]
+        return copy(k, way, place, place, mate)
+
+    def keep(k):
+        return pltpu.make_async_copy(source(order[k]), slot(order[k], me), local_sem.at[k])
+
+    def project(c):
+        depth = weights.shape[1] * weights.shape[2]
+        w = weights[c].reshape(depth, weights.shape[3])
+        return jnp.dot(x_ref[...], w, preferred_element_type=jnp.float32).astype(jnp.bfloat16)
+
+    def finish(k):
+        kind, c = order[k]
+        for way in (0, 5, 6, 7):
+            arrival(k, way).wait_recv()
+        keep(k).wait()
+        if kind == "kv":
+            return
+        y = project(c)
+        if c < kinds:
+            own_kv[c] = y
+            return
+        expert = c - kinds
+        for s in range(q_ref.shape[0]):
+            mine = routes_ref[:, s : s + 1] == expert
+            before = jnp.zeros_like(y) if expert == 0 else q_ref[s]
+            q_ref[s] = jnp.where(mine, y, before)
+
+    for k in range(count + 3):
+        if k < count:
+            for way in (1, 2, 0):
+                send(k, way).start()
+            keep(k).start()
+        j = k - 1
+        if 0 <= j < count:
+            arrival(j, 1).wait_recv()
+            send(j, 4).start()
+            send(j, 5).start()
+            arrival(j, 2).wait_recv()
+            send(j, 3).start()
+            send(j, 6).start()
+        j = k - 2
+        if 0 <= j < count:
+            arrival(j, 3).wait_recv()
+            arrival(j, 4).wait_recv()
+            send(j, 7).start()
+        j = k - 3
+        if 0 <= j < count:
+            finish(j)
+    for k in range(count):
+        for way in range(8):
+            send(k, way).wait_send()
+
+
+def gather_project(normed, routes, kv_weight, query_weight, shards):
+    tokens, width = normed.shape
+    kinds, rows, cols = kv_weight.shape
+    experts = query_weight.shape[0]
+    slots = routes.shape[1]
+    chunks = 2 * kinds + experts
+    vmem = pl.BlockSpec(memory_space=pltpu.VMEM)
+    anywhere = pl.BlockSpec(memory_space=pl.ANY)
+    return pl.pallas_call(
+        gather_kernel,
+        in_specs=[vmem, vmem, anywhere, anywhere],
+        out_specs=[vmem, anywhere],
+        out_shape=[
+            jax.ShapeDtypeStruct((slots, tokens, cols), jnp.bfloat16),
+            jax.ShapeDtypeStruct((shards, kinds, tokens, cols), jnp.bfloat16),
+        ],
+        scratch_shapes=[
+            pltpu.VMEM((kinds + experts, shards, rows, cols), jnp.bfloat16),
+            pltpu.VMEM((kinds, tokens, cols), jnp.bfloat16),
+            pltpu.SemaphoreType.DMA((chunks, 8)),
+            pltpu.SemaphoreType.DMA((chunks, 8)),
+            pltpu.SemaphoreType.DMA((chunks,)),
+        ],
+        compiler_params=pltpu.CompilerParams(
+            collective_id=1, has_side_effects=True, vmem_limit_bytes=VMEM_BYTES
+        ),
+        cost_estimate=pl.CostEstimate(
+            flops=2 * (kinds + experts) * tokens * width * cols * 10,
+            bytes_accessed=200 * 1024 * 1024,
+            transcendentals=0,
+        ),
+        name="gather_project",
+    )(normed, routes, kv_weight, query_weight)
+
+
+def out_sum_kernel(
+    x_ref,
+    routes_ref,
+    gates_ref,
+    hidden_ref,
+    w_ref,
+    out_ref,
+    weights,
+    picked,
+    own,
+    near,
+    far,
+    load_sem,
+    send_sem,
+    recv_sem,
+):
+    me = lax.axis_index("mdl")
+    low, high = me % 2, me // 2
+    near_id, far_id = me + 1 - 2 * low, me + 2 - 4 * high
+    both = near_id + 2 - 4 * high
+    shards, experts = w_ref.shape[:2]
+    cols = w_ref.shape[3]
+    per = shards // 4
+    targets = [both, near_id, far_id, me]
+
+    def load(n):
+        index = targets[n // per] * per + n % per
+        return pltpu.make_async_copy(w_ref.at[index], weights.at[n], load_sem.at[n])
+
+    for n in range(shards):
+        load(n).start()
+
+    barrier = pltpu.get_barrier_semaphore()
+    for other in (near_id, far_id):
+        pl.semaphore_signal(
+            barrier, inc=1, device_id={"mdl": other}, device_id_type=pl.DeviceIdType.MESH
+        )
+    pl.semaphore_wait(barrier, 2)
+
+    for e in range(experts):
+        rows = jnp.zeros_like(x_ref[0])
+        for s in range(x_ref.shape[0]):
+            rows = jnp.where(routes_ref[:, s : s + 1] == e, x_ref[s], rows)
+        picked[e] = rows
+
+    def copy(way, src, dst, other):
+        return pltpu.make_async_remote_copy(
+            src_ref=src,
+            dst_ref=dst,
+            send_sem=send_sem.at[way],
+            recv_sem=recv_sem.at[way],
+            device_id={"mdl": other},
+            device_id_type=pl.DeviceIdType.MESH,
+        )
+
+    def near_copy(way):
+        return copy(way, own.at[way], near.at[way], near_id)
+
+    def far_copy():
+        return copy(2, own.at[2], far, far_id)
+
+    def block(n, piece):
+        load(n * per + piece).wait()
+        total = jnp.zeros((own.shape[1], cols), jnp.float32)
+        for e in range(experts):
+            term = jnp.dot(picked[e], weights[n * per + piece, e], preferred_element_type=jnp.float32)
+            total = total + gates_ref[:, e : e + 1] * term
+        return total
+
+    for n in range(4):
+        for piece in range(per):
+            span = slice(piece * cols, (piece + 1) * cols)
+            own[n, :, span] = block(n, piece).astype(jnp.bfloat16)
+        if n < 2:
+            near_copy(n).start()
+        elif n == 2:
+            near_copy(0).wait_recv()
+            own[2] = (own[2].astype(jnp.float32) + near[0].astype(jnp.float32)).astype(jnp.bfloat16)
+            far_copy().start()
+    near_copy(1).wait_recv()
+    part = own[3].astype(jnp.float32) + near[1].astype(jnp.float32) + hidden_ref[...].astype(jnp.float32)
+    far_copy().wait_recv()
+    out_ref[...] = (part + far[...].astype(jnp.float32)).astype(jnp.bfloat16)
+    near_copy(0).wait_send()
+    near_copy(1).wait_send()
+    far_copy().wait_send()
+
+
+def project_out_sum(attended, routes, gates, residual, weight):
+    shards, experts, rows, cols = weight.shape
+    _, tokens, _ = attended.shape
+    span = shards * cols // 4
+    vmem = pl.BlockSpec(memory_space=pltpu.VMEM)
+    return pl.pallas_call(
+        out_sum_kernel,
+        in_specs=[vmem, vmem, vmem, vmem, pl.BlockSpec(memory_space=pl.ANY)],
+        out_specs=vmem,
+        out_shape=jax.ShapeDtypeStruct((tokens, span), jnp.bfloat16),
+        scratch_shapes=[
+            pltpu.VMEM((shards, experts, rows, cols), jnp.bfloat16),
+            pltpu.VMEM((experts, tokens, rows), jnp.bfloat16),
+            pltpu.VMEM((4, tokens, span), jnp.bfloat16),
+            pltpu.VMEM((2, tokens, span), jnp.bfloat16),
+            pltpu.VMEM((tokens, span), jnp.bfloat16),
+            pltpu.SemaphoreType.DMA((shards,)),
+            pltpu.SemaphoreType.DMA((3,)),
+            pltpu.SemaphoreType.DMA((3,)),
+        ],
+        compiler_params=pltpu.CompilerParams(
+            collective_id=2, has_side_effects=True, vmem_limit_bytes=VMEM_BYTES
+        ),
+        cost_estimate=pl.CostEstimate(
+            flops=2 * experts * tokens * rows * shards * cols,
+            bytes_accessed=2 * weight.size,
+            transcendentals=0,
+        ),
+        name="project_out_sum",
+    )(attended, routes, gates, residual, weight)
+
+
 def local(
     hidden,
     segment_ids,
@@ -269,13 +559,18 @@
     pages_here = page_table.shape[0]
     page_rows = tok_dev // pages_here
 
-    kv_full = lax.all_gather(kv_weight, "tok", axis=0)
+    own_kernels = shards == 8 and parts == 4
     table = lax.all_gather(page_table, "tok", axis=0, tiled=True)
     normed = rms_norm(hidden, norm_gain)
     gates = route_gates(normed, router_weight, routes)
-    key_values = lax.all_gather(project_kv(normed, kv_full), "tok", axis=0)
-    query_full = lax.all_gather(query_weight, "tok", axis=0)
     out_full = lax.all_gather(out_weight, "tok", axis=0)
+    if own_kernels:
+        queries, key_values = gather_project(normed, routes, kv_weight, query_weight, shards)
+    else:
+        kv_full = lax.all_gather(kv_weight, "tok", axis=0)
+        key_values = lax.all_gather(project_kv(normed, kv_full), "tok", axis=0)
+        query_full = lax.all_gather(query_weight, "tok", axis=0)
+        queries = project_queries(normed, routes, query_full)
 
     here = tok_row * pages_here + jnp.arange(pages_here, dtype=jnp.int32)
     logical = jnp.arange(table.shape[0], dtype=jnp.int32)
@@ -291,12 +586,13 @@
         jnp.where(own_seg[:, None] == prompt_ids[None, :], seg_first[None, :], 0), axis=1
     )
 
-    queries = project_queries(normed, routes, query_full)
     attended = attend(queries, lower, key_values, first)
+    span = width // parts
+    residual = lax.dynamic_slice_in_dim(hidden, lax.axis_index("mdl") * span, span, 1)
+    if own_kernels:
+        return (project_out_sum(attended, routes, gates, residual, out_full), cache)
     partial_sums = project_out(attended, routes, gates, out_full, parts)
     mine = lax.psum_scatter(partial_sums, "mdl", scatter_dimension=0, tiled=False)
-    span = width // parts
-    residual = lax.dynamic_slice_in_dim(hidden, lax.axis_index("mdl") * span, span, 1)
     output = (residual.astype(jnp.float32) + mine.astype(jnp.float32)).astype(jnp.bfloat16)
     return (output, cache)
 

time: 358 us -> 297 us (0.83)
  the two profiles are of different devices: /device:TPU:0 before, /device:TPU:6 now
where the time goes in v2:
time: 297 us; the launch traced here: 291 us
  Pallas kernels  250 us (84%)
  local copies, waits for them, and re-layouts  15.6 us (5%)
  between operations  15 us (5%)
  blocking collectives  6.37 us (2%)
    pallas_call x1, Pallas kernels, gather_project(): pl.pallas_call(gather_kernel, in_specs=[vmem, vmem, anywhere, anywhere],...  189 us
    pallas_call x1, Pallas kernels, project_out_sum(): pl.pallas_call(out_sum_kernel, in_specs=[vmem, vmem, vmem, vmem, pl.Block...  38.1 us
    pallas_call x1, Pallas kernels, attend(): pl.pallas_call(functools.partial(attention_kernel, block_k=block_k, heads...  22.1 us
    unnamed x34, local copies, waits for them, and re-layouts  10.2 us
    unnamed x1, blocking collectives  6.37 us
  transfers between devices with their start and end apart: 1, of which 0 were waited for; matrix products, arithmetic and copies ran while one was open for 4% of the time, Pallas kernels for 73%

profile of v2, /device:TPU:6, one launch (start us, length us, event | category | flops | bytes accessed | tf_op | source)
XLA Modules:
  0.0 290.8 jit_solution(12611995300830408318)
XLA Ops:
  7.2 0.0 copy-start
  7.2 0.0 copy-start.10
  7.2 0.0 copy-start.9
  7.2 0.0 copy-start.7
  7.2 0.0 copy-start.11
  7.2 0.0 all-gather.3.cloned.1.call-start
  7.3 0.7 all-gather.3.cloned.1.call-update
  8.0 0.0 copy-done.10
  8.0 0.1 dynamic_slice.6
  8.1 0.1 convert_reduce_fusion
  8.2 0.1 select_reduce_fusion.3
  8.3 0.1 fusion.11
  8.4 0.1 pad_add_fusion
  8.5 0.1 reshape.158
  8.5 0.0 copy-done.9
  8.6 0.1 copy.25.routes_ref
  8.7 0.1 copy-done.7
  8.8 0.5 fusion
  9.3 0.0 copy-done.11
  9.3 1.1 copy-done.8
  10.4 0.5 fusion.2.x_ref
  11.0 0.0 copy-done
  11.0 0.0 copy-start.13
  11.0 0.0 copy-start.12
  11.0 0.0 copy-start.2
  11.0 1.7 fusion.12
  12.9 0.1 copy.27.gates_ref
  13.0 0.0 copy-done.13
  13.0 0.6 dynamic-slice
  14.3 0.0 copy-done.12
  14.3 0.2 dynamic-update-slice
  14.5 6.4 %all-reduce = s32[256]{0:T(256)S(1)} all-reduce(s32[256]{0:T(256)S(1)} %dynamic-update-slice), channel_id=1, replica_groups=mesh['tok'=8,'mdl'=4] {'tok'}, use_global_device_ids=true, to_apply=%add | all-reduce | flops 256 | bytes 2048
  20.9 0.2 select_reduce_fusion
  21.1 0.0 copy-done.2
  21.1 0.0 copy-start.1
  21.1 1.8 copy-done.1
  22.9 189.5 %gather_project.1 = (bf16[2,512,512]{2,1,0:T(8,128)(2,1)S(1)}, bf16[8,2,512,512]{3,2,1,0:T(8,128)(2,1)}) custom-call(bf16[512,2048]{1,0:T(8,128)(2,1)S(1)} %fusion.2.x_ref, s32[512,2]{1,0:T(8,128)S(1)} %copy.25.routes_ref, bf16[2,256,512]{2,1,0:T(8,128)(2,1)S(1)} %copy-done.2, bf16[8,256,512]{2,1,0:T(8,128)(2,1)S(1)} %copy-done.1), custom_call_target="tpu_custom_call" | custom-call | flops 107374182400 | bytes 209715200 | tf_op jit(solution)/shard_map/gather_project/pallas_call | solution.py:396
  212.4 0.0 copy-start.3
  212.4 1.1 copy-done.3
  213.5 4.0 %gather_fusion = bf16[32,2,16,512]{3,2,1,0:T(8,128)(2,1)S(1)} fusion(bf16[8,2,32,16,512]{4,3,2,1,0:T(8,128)(2,1)} %bitcast.27, s32[32]{0:T(128)S(1)} %fusion.10), kind=kCustom, calls=%fused_computation | custom fusion | bytes 2097408 | tf_op jit(solution)/shard_map/gather | solution.py:579
  217.5 2.1 copy.28
  219.5 0.1 pad_add_fusion.1.bounds_ref
  219.6 1.1 constant_dynamic-slice_fusion.hidden_ref
  220.7 22.1 %attend.1.x_ref = bf16[2,512,512]{2,1,0:T(8,128)(2,1)S(1)} custom-call(s32[5]{0:T(128)S(1)} %pad_add_fusion.1.bounds_ref, bf16[2,512,512]{2,1,0:T(8,128)(2,1)S(1)} %copy-done.4, s32[2,1,256]{2,1,0:T(1,128)S(1)} %bitcast.25, bf16[8,2,512,512]{3,2,1,0:T(8,128)(2,1)} %get-tuple-element.5.kv_ref), custom_call_target="tpu_custom_call" | custom-call | flops 4294967296 | bytes 10485760 | tf_op jit(solution)/shard_map/attend/pallas_call | solution.py:185
  242.9 1.0 copy-done.5
  243.9 1.2 copy-done.6
  245.1 38.1 %project_out_sum.1 = bf16[512,512]{1,0:T(8,128)(2,1)S(1)} custom-call(bf16[2,512,512]{2,1,0:T(8,128)(2,1)S(1)} %copy-done.6, s32[512,2]{1,0:T(8,128)S(1)} %copy.25.routes_ref, f32[512,8]{1,0:T(8,128)S(1)} %copy.27.gates_ref, bf16[512,512]{1,0:T(8,128)(2,1)S(1)} %constant_dynamic-slice_fusion.hidden_ref, bf16[8,8,512,256]{3,2,1,0:T(8,128)(2,1)} %bitcast.28), custom_call_target="tpu_custom_call" | custom-call | flops 8589934592 | bytes 16777216 | tf_op jit(solution)/shard_map/project_out_sum/pallas_call | solution.py:516
  283.1 0.8 copy.31
  (16 shorter events, 0.2 us)
Async XLA Ops:
  7.2 3.8 %copy-start = (f32[2048,8]{0,1:T(8,128)S(1)}, f32[2048,8]{0,1:T(8,128)}, u32[]{:S(2)}) copy-start(f32[2048,8]{0,1:T(8,128)} %param.13) | copy-start | bytes 196612
  7.2 0.8 copy-start.10
  7.2 1.4 copy-start.9
  7.2 1.6 copy-start.7
  7.2 2.1 copy-start.11
  7.2 236.6 %all-gather.3.cloned.1.call-start = ((), (), s32[]{:S(2)}) async-start(), calls=%async_computation | async-start | bytes 18874368 | tf_op jit(solution)/shard_map/all_gather | solution.py:566
  8.8 1.6 copy-start.8
  11.0 2.0 copy-start.13
  11.0 3.3 %copy-start.12 = (s32[32]{0:T(128)S(1)}, s32[32]{0:T(128)}, u32[]{:S(2)}) copy-start(s32[32]{0:T(128)} %param.17) | copy-start | bytes 388
  11.0 10.1 %copy-start.2 = (bf16[2,256,512]{2,1,0:T(8,128)(2,1)S(1)}, bf16[2,256,512]{2,1,0:T(8,128)(2,1)}, u32[]{:S(2)}) copy-start(bf16[2,256,512]{2,1,0:T(8,128)(2,1)} %kvw_ref.1) | copy-start | bytes 1572868
  21.1 1.8 copy-start.1
  212.4 1.1 copy-start.3
  217.5 3.2 %copy-start.4 = (bf16[2,512,512]{2,1,0:T(8,128)(2,1)S(1)}, bf16[2,512,512]{2,1,0:T(8,128)(2,1)}, u32[]{:S(2)}) copy-start(bf16[2,512,512]{2,1,0:T(8,128)(2,1)} %copy-done.3) | copy-start | bytes 3145732
  242.9 1.0 copy-start.5
  243.9 1.2 copy-start.6
Sparse Core Ops, SparseCore 0:
  9.9 155.4 all-gather.2
